TPU v7x, 32 devices: a whole 2x2x4 slice. The times are simulated.
32 devices in a mesh: quad: 8 (over z, x), conf: 4 (over y, core).
Axes of the slice: x: 2, y: 2, z: 4, core: 2. Of those that a mesh axis runs over, the one named last changes fastest.
Arguments:
- configs: bfloat16 [8192, 6144], P('conf', 'quad'), may hold values from -0.078125 to 0.078125
- weights: float32 [6144], P('quad'), may hold values from 0.5 to 2
Outputs:
- shell_matrix: float32 [8192, 8192], P('quad', 'conf')
All inputs are finite; a program needn't handle non-finite values.
Results may differ from a plain program's by a relative error of at most 0.0085.
Values may be sent and summed in bfloat16 or wider, within the bound.
A program may use at most 128 MiB of HBM per device.

v0:
```python
import jax
import jax.numpy as jnp
from jax import lax
from jax.sharding import PartitionSpec as P


def pair_product(left, right):
    return lax.dot_general(
        left, right, (((1,), (1,)), ((), ())), preferred_element_type=jnp.float32
    )


def local(configs, weights):
    gathered = lax.all_gather(configs, "conf", axis=0, tiled=True)
    scaled = (gathered.astype(jnp.float32) * weights[None, :]).astype(jnp.bfloat16)
    return lax.psum_scatter(pair_product(scaled, configs), "quad", scatter_dimension=0, tiled=True)


def solution(mesh):
    return jax.shard_map(
        local,
        mesh=mesh,
        in_specs=(P("conf", "quad"), P("quad")),
        out_specs=P("quad", "conf"),
        check_vma=False,
    )
```

profile of v0, /device:TPU:24, one launch (start us, length us, event | category | flops | bytes accessed | tf_op | source)
XLA Modules:
  0.0 1191.0 jit_solution(8121258883205355384)
XLA Ops:
  6.5 0.0 all-gather.2.cloned.1.call-start
  6.5 0.7 all-gather.2.cloned.1.call-update
  7.3 0.0 reduce-scatter.2.cloned.1.call-start
  7.3 84.7 %all-gather.2.cloned.1.call-done = bf16[8192,768]{1,0:T(8,128)(2,1)} async-done(((bf16[2048,768]{1,0:T(8,128)(2,1)}), bf16[8192,768]{1,0:T(8,128)(2,1)}) %all-gather.2.cloned.1.call-update) | async-done | bytes 12582928 | tf_op jit(solution)/shard_map/all_gather | solution.py:14
  92.0 35.6 %fusion = f32[8192,2048]{1,0:T(8,128)} fusion(bf16[2048,768]{1,0:T(8,128)(2,1)} %param.2, bf16[8192,768]{1,0:T(8,128)(2,1)} %all-gather.2.cloned.1.call-done, f32[768]{0:T(1024)} %param.3), kind=kOutput, calls=%fused_computation.1 | convolution fusion | flops 25788678144 | bytes 82840576 | tf_op jit(solution)/shard_map/dot_general | solution.py:8
  127.7 0.0 reduce-scatter.2.cloned.1.call-update
  127.7 1056.5 %reduce-scatter.2.cloned.1.call-done = f32[1024,2048]{1,0:T(8,128)} async-done(((f32[8192,2048]{1,0:T(8,128)}), f32[1024,2048]{1,0:T(8,128)}) %reduce-scatter.2.cloned.1.call-update) | async-done | bytes 8388624 | tf_op jit(solution)/shard_map/reduce_scatter | solution.py:16
Async XLA Ops:
  6.5 85.5 %all-gather.2.cloned.1.call-start = ((), (), s32[]{:S(2)}) async-start(), calls=%async_computation.1 | async-start | bytes 15728640 | tf_op jit(solution)/shard_map/all_gather | solution.py:14
  7.3 1176.9 %reduce-scatter.2.cloned.1.call-start = ((), (), s32[]{:S(2)}) async-start(), calls=%async_computation.2 | async-start | bytes 75497472 | tf_op jit(solution)/shard_map/reduce_scatter | solution.py:16
Sparse Core Ops, SparseCore 0:
  8.9 83.0 all-gather.1
  127.8 1056.3 reduce-scatter.1
where the time goes:
time: 1190 us
  waiting for transfers between devices  1140 us (96%)
  matrix products  35.6 us (3%)
  between operations  13.4 us (1%)
    reduce_scatter x1, waiting for transfers between devices, local(): lax.psum_scatter(pair_product(scaled, configs), 'quad', scatter_dimension...  1060 us
    all_gather x1, waiting for transfers between devices, local(): gathered = lax.all_gather(configs, 'conf', axis=0, tiled=True)  84.7 us
    dot_general x1, matrix products, pair_product(): lax.dot_general(left, right, (((1,), (1,)), ((), ())), preferred_element_...  35.6 us
  transfers between devices with their start and end apart: 2, of which 2 were waited for; matrix products, arithmetic and copies ran while one was open for 0% of the time, Pallas kernels for 0%

commit v1 on v0

v1 whole, which is shorter than its diff:
```python
import functools

import jax
import jax.numpy as jnp
from jax import lax
from jax.experimental import pallas as pl
from jax.experimental.pallas import tpu as pltpu
from jax.sharding import PartitionSpec as P

MESH = pl.DeviceIdType.MESH


def visit(z, k, nz):
    below, above = z, nz - 1 - z
    pairs = jnp.minimum(below, above)
    paired = k <= 2 * pairs
    step = jnp.where(paired, (k + 1) // 2, k - pairs)
    down = jnp.where(paired, k % 2 == 1, below > above)
    return jnp.where(down, z - step, z + step)


def kernel(nq, nc, x_ref, w_ref, out_ref, held, left, wts, scaled,
           load_sem, recv_sem, line_sem, own_sem, pair_sem, left_recv, left_send, w_recv, w_send):
    chunks, rows, _ = x_ref.shape
    nz = nq // 2
    q, c = lax.axis_index("quad"), lax.axis_index("conf")
    z, x = q // 2, q % 2
    root, mine = q // chunks, q % chunks
    bits = nc.bit_length() - 1
    far = 0
    for b in range(bits):
        far = far + (((c // 2**b) % 2 + (root // 2**b) % 2) % 2) * 2**b

    load = pltpu.make_async_copy(x_ref, held.at[q], load_sem)
    load.start()
    barrier = pltpu.get_barrier_semaphore()
    for k in range(1, nq):
        pl.semaphore_signal(barrier, inc=1, device_id={"quad": lax.rem(q + k, nq)}, device_id_type=MESH)
    for k in range(1, nc):
        pl.semaphore_signal(barrier, inc=1, device_id={"conf": lax.rem(c + k, nc)}, device_id_type=MESH)
    wts[q] = jnp.broadcast_to(w_ref[...], wts.shape[1:])
    load.wait()
    pl.semaphore_wait(barrier, nq + nc - 2)

    def along(slot, ch, to, sem):
        return pltpu.make_async_remote_copy(
            src_ref=held.at[slot, ch], dst_ref=held.at[slot, ch], send_sem=sem,
            recv_sem=recv_sem.at[slot, ch], device_id={"quad": to}, device_id_type=MESH)

    def line_copy(slot, ch, to):
        return along(slot, ch, to, line_sem.at[slot // 2, ch])

    def own_copy(ch, to):
        return along(q, ch, to, own_sem.at[ch])

    def pair_copy(slot, ch):
        return along(slot, ch, 2 * z + 1 - x, pair_sem.at[slot // 2, ch])

    def left_copy(src, slot, b):
        bit = (c // 2**b) % 2
        return pltpu.make_async_remote_copy(
            src_ref=src, dst_ref=left.at[slot], send_sem=left_send.at[slot, b],
            recv_sem=left_recv.at[slot], device_id={"conf": c + (1 - 2 * bit) * 2**b}, device_id_type=MESH)

    def weight_copy(k):
        return pltpu.make_async_remote_copy(
            src_ref=wts.at[q], dst_ref=wts.at[q], send_sem=w_send.at[k],
            recv_sem=w_recv.at[q], device_id={"quad": lax.rem(q + k, nq)}, device_id_type=MESH)

    def pass_left(src, slot, here):
        for b in reversed(range(bits)):
            @pl.when(jnp.logical_and(here, far % 2 ** (b + 1) == 0))
            def _():
                left_copy(src, slot, b).start()

    def root_sends(slot, ch):
        pass_left(held.at[slot, ch], slot, jnp.logical_and(far == 0, ch == mine))

    def turn(ch, source):
        return (ch + 1 - source) % chunks

    for i in range(chunks):
        ch = turn(i, x)

        @pl.when(z < nz - 1)
        def _():
            line_copy(q, ch, q + 2).start()

        @pl.when(z > 0)
        def _():
            own_copy(ch, q - 2).start()

        pair_copy(q, ch).start()
        root_sends(q, ch)
    for k in range(1, nq):
        weight_copy(k).start()

    out_ref[...] = jnp.zeros_like(out_ref)

    def multiply(slot):
        @pl.when(slot != q)
        def _():
            weight_copy_from = pltpu.make_async_remote_copy(
                src_ref=wts.at[slot], dst_ref=wts.at[slot], send_sem=w_send.at[0],
                recv_sem=w_recv.at[slot], device_id={"quad": lax.rem(q + 1, nq)}, device_id_type=MESH)
            weight_copy_from.wait_recv()

        scale = wts[slot, 0:1, :]

        @pl.when(far != 0)
        def _():
            left_copy(left.at[slot], slot, 0).wait_recv()
            pass_left(left.at[slot], slot, True)
            scaled[...] = (left[slot].astype(jnp.float32) * scale).astype(jnp.bfloat16)

        @pl.when(far == 0)
        def _():
            scaled[...] = (held[slot, mine].astype(jnp.float32) * scale).astype(jnp.bfloat16)

        tile = min(256, rows)
        for ch in range(chunks):
            @pl.loop(0, rows // tile)
            def _(t):
                part = pl.ds(pl.multiple_of(t * tile, tile), tile)
                out_ref[part, ch * rows:(ch + 1) * rows] += lax.dot_general(
                    scaled[part, :], held[slot, ch], (((1,), (1,)), ((), ())),
                    preferred_element_type=jnp.float32)

    @pl.loop(1, nz + 2)
    def _(k):
        at = visit(z, jnp.minimum(k, nz - 1), nz)
        slot = 2 * at + x
        before = visit(z, jnp.clip(k - 1, 0, nz - 1), nz)
        for i in range(chunks):
            @pl.when(k < nz)
            def _():
                ch = turn(i, x)
                line_copy(slot, ch, q).wait_recv()

                @pl.when(jnp.logical_and(at < z, z < nz - 1))
                def _():
                    line_copy(slot, ch, q + 2).start()

                @pl.when(jnp.logical_and(at > z, z > 0))
                def _():
                    line_copy(slot, ch, q - 2).start()

                pair_copy(slot, ch).start()
                root_sends(slot, ch)

            @pl.when(k <= nz)
            def _():
                ch = turn(i, 1 - x)
                other = 2 * before + 1 - x
                line_copy(other, ch, q).wait_recv()
                root_sends(other, ch)

        @pl.when(k <= nz)
        def _():
            multiply(2 * before + x)

        @pl.when(k >= 2)
        def _():
            multiply(2 * visit(z, jnp.maximum(k - 2, 0), nz) + 1 - x)

    for ch in range(chunks):
        @pl.when(z > 0)
        def _():
            own_copy(ch, q - 2).wait_send()

    @pl.loop(0, nz)
    def _(at):
        for ch in range(chunks):
            slot = 2 * at + x
            sent = jnp.logical_or(jnp.logical_and(at <= z, z < nz - 1), jnp.logical_and(at > z, z > 0))

            @pl.when(sent)
            def _():
                line_copy(slot, ch, q).wait_send()

            pair_copy(slot, ch).wait_send()

    @pl.loop(0, nq)
    def _(slot):
        for b in range(bits):
            @pl.when(far % 2 ** (b + 1) == 0)
            def _():
                left_copy(left.at[slot], slot, b).wait_send()

    for k in range(1, nq):
        weight_copy(k).wait_send()


def local(nq, nc, configs, weights):
    columns, width = configs.shape
    rows = columns * nc // nq
    chunks = columns // rows
    dma = pltpu.SemaphoreType.DMA
    bits = nc.bit_length() - 1
    return pl.pallas_call(
        functools.partial(kernel, nq, nc),
        out_shape=jax.ShapeDtypeStruct((rows, columns), jnp.float32),
        in_specs=[pl.BlockSpec(memory_space=pl.ANY), pl.BlockSpec(memory_space=pltpu.VMEM)],
        out_specs=pl.BlockSpec(memory_space=pltpu.VMEM),
        scratch_shapes=[
            pltpu.VMEM((nq, chunks, rows, width), jnp.bfloat16),
            pltpu.VMEM((nq, rows, width), jnp.bfloat16),
            pltpu.VMEM((nq, 8, width), jnp.float32),
            pltpu.VMEM((rows, width), jnp.bfloat16),
            dma,
            dma((nq, chunks)),
            dma((nq // 2, chunks)),
            dma((chunks,)),
            dma((nq // 2, chunks)),
            dma((nq,)),
            dma((nq, bits)),
            dma((nq,)),
            dma((nq,)),
        ],
        compiler_params=pltpu.CompilerParams(
            collective_id=0, has_side_effects=True, vmem_limit_bytes=60 * 2**20),
        cost_estimate=pl.CostEstimate(
            flops=2 * rows * columns * width * nq, transcendentals=0,
            bytes_accessed=2 * columns * width + 4 * rows * columns),
    )(configs.reshape(chunks, rows, width), weights.reshape(1, width))


def solution(mesh):
    return jax.shard_map(
        functools.partial(local, mesh.shape["quad"], mesh.shape["conf"]),
        mesh=mesh,
        in_specs=(P("conf", "quad"), P("quad")),
        out_specs=P("quad", "conf"),
        check_vma=False,
    )
```

time: 1190 us -> 311 us (0.26)
  waiting for transfers between devices: 1140 us -> 0 us
  Pallas kernels: 0 us -> 298 us
  matrix products: 35.6 us -> 0 us
  between operations: 13.4 us -> 0.01 us
    reduce_scatter x1 -> x0, waiting for transfers between devices: 1060 us -> none  [local(): lax.psum_scatter(pair_product(scaled, configs), 'quad', scatter_dimension...]
    pallas_call x0 -> x1, Pallas kernels: none -> 298 us  [local(): pl.pallas_call(functools.partial(kernel, nq, nc), out_shape=jax.ShapeDtyp...]
    all_gather x1 -> x0, waiting for transfers between devices: 84.7 us -> none  [local(): gathered = lax.all_gather(configs, 'conf', axis=0, tiled=True)]
    dot_general x1 -> x0, matrix products: 35.6 us -> none  [pair_product(): lax.dot_general(left, right, (((1,), (1,)), ((), ())), preferred_element_...]
  transfers between devices with their start and end apart: 2 -> 0, of which waited for: 2 -> 0; matrix products, arithmetic and copies ran while one was open for 0% -> 0% of each run, Pallas kernels for 0% -> 0%
where the time goes in v1:
time: 311 us; the launch traced here: 308 us
  Pallas kernels  298 us (96%)
  local copies, waits for them, and re-layouts  9.15 us (3%)
    pallas_call x1, Pallas kernels, local(): pl.pallas_call(functools.partial(kernel, nq, nc), out_shape=jax.ShapeDtyp...  298 us
    unnamed x1, local copies, waits for them, and re-layouts  7.89 us

profile of v1, /device:TPU:24, one launch (start us, length us, event | category | flops | bytes accessed | tf_op | source)
XLA Modules:
  0.0 307.6 jit_solution(8470880161228019919)
XLA Ops:
  0.0 1.3 reshape.7.w_ref
  1.3 298.5 %shard_map.28 = f32[1024,2048]{1,0:T(8,128)} custom-call(bf16[2,1024,768]{2,1,0:T(8,128)(2,1)} %bitcast.1, f32[1,768]{1,0:T(1,128)} %reshape.7.w_ref), custom_call_target="tpu_custom_call" | custom-call | flops 25769803776 | bytes 11534336 | tf_op jit(solution)/shard_map/pallas_call | solution.py:200
  299.8 7.9 %copy.4 = f32[1024,2048]{1,0:T(8,128)} copy(f32[1024,2048]{1,0:T(8,128)} %shard_map.28) | data formatting | bytes 16777216

commit v2 on v1

--- a/solution.py
+++ b/solution.py
@@ -20,12 +20,13 @@
 
 
 def kernel(nq, nc, x_ref, w_ref, out_ref, held, left, wts, scaled,
-           load_sem, recv_sem, line_sem, own_sem, pair_sem, left_recv, left_send, w_recv, w_send):
+           load_sem, recv_sem, line_sem, own_sem, pair_sem, cross_sem, left_recv, left_send, w_recv, w_send):
     chunks, rows, _ = x_ref.shape
     nz = nq // 2
     q, c = lax.axis_index("quad"), lax.axis_index("conf")
     z, x = q // 2, q % 2
     root, mine = q // chunks, q % chunks
+    buddy = z + 1 - 2 * (z % 2)
     bits = nc.bit_length() - 1
     far = 0
     for b in range(bits):
@@ -38,7 +39,7 @@
         pl.semaphore_signal(barrier, inc=1, device_id={"quad": lax.rem(q + k, nq)}, device_id_type=MESH)
     for k in range(1, nc):
         pl.semaphore_signal(barrier, inc=1, device_id={"conf": lax.rem(c + k, nc)}, device_id_type=MESH)
-    wts[q] = jnp.broadcast_to(w_ref[...], wts.shape[1:])
+    wts[q] = jnp.broadcast_to(w_ref[...].reshape(1, -1), wts.shape[1:])
     load.wait()
     pl.semaphore_wait(barrier, nq + nc - 2)
 
@@ -55,6 +56,9 @@
 
     def pair_copy(slot, ch):
         return along(slot, ch, 2 * z + 1 - x, pair_sem.at[slot // 2, ch])
+
+    def cross_copy(at):
+        return along(2 * at + 1 - x, turn(chunks - 1, 1 - x), 2 * buddy + x, cross_sem)
 
     def left_copy(src, slot, b):
         bit = (c // 2**b) % 2
@@ -126,6 +130,9 @@
                     scaled[part, :], held[slot, ch], (((1,), (1,)), ((), ())),
                     preferred_element_type=jnp.float32)
 
+    def paired(at, i):
+        return jnp.logical_or(at != buddy, i < chunks - 1)
+
     @pl.loop(1, nz + 2)
     def _(k):
         at = visit(z, jnp.minimum(k, nz - 1), nz)
@@ -145,23 +152,39 @@
                 def _():
                     line_copy(slot, ch, q - 2).start()
 
-                pair_copy(slot, ch).start()
+                @pl.when(paired(at, i))
+                def _():
+                    pair_copy(slot, ch).start()
+
                 root_sends(slot, ch)
 
-            @pl.when(k <= nz)
+            @pl.when(jnp.logical_and(k <= nz, paired(before, i)))
             def _():
                 ch = turn(i, 1 - x)
                 other = 2 * before + 1 - x
                 line_copy(other, ch, q).wait_recv()
                 root_sends(other, ch)
 
+            if i == 0:
+                @pl.when(k == nz)
+                def _():
+                    cross_copy(z).start()
+
         @pl.when(k <= nz)
         def _():
             multiply(2 * before + x)
 
-        @pl.when(k >= 2)
-        def _():
-            multiply(2 * visit(z, jnp.maximum(k - 2, 0), nz) + 1 - x)
+        last = visit(z, jnp.maximum(k - 2, 0), nz)
+
+        @pl.when(jnp.logical_and(k >= 2, last != buddy))
+        def _():
+            multiply(2 * last + 1 - x)
+
+    other = 2 * buddy + 1 - x
+    cross_copy(buddy).wait_recv()
+    root_sends(other, turn(chunks - 1, 1 - x))
+    multiply(other)
+    cross_copy(z).wait_send()
 
     for ch in range(chunks):
         @pl.when(z > 0)
@@ -170,7 +193,8 @@
 
     @pl.loop(0, nz)
     def _(at):
-        for ch in range(chunks):
+        for i in range(chunks):
+            ch = turn(i, x)
             slot = 2 * at + x
             sent = jnp.logical_or(jnp.logical_and(at <= z, z < nz - 1), jnp.logical_and(at > z, z > 0))
 
@@ -178,7 +202,9 @@
             def _():
                 line_copy(slot, ch, q).wait_send()
 
-            pair_copy(slot, ch).wait_send()
+            @pl.when(paired(at, i))
+            def _():
+                pair_copy(slot, ch).wait_send()
 
     @pl.loop(0, nq)
     def _(slot):
@@ -212,6 +238,7 @@
             dma((nq // 2, chunks)),
             dma((chunks,)),
             dma((nq // 2, chunks)),
+            dma,
             dma((nq,)),
             dma((nq, bits)),
             dma((nq,)),
@@ -222,7 +249,7 @@
         cost_estimate=pl.CostEstimate(
             flops=2 * rows * columns * width * nq, transcendentals=0,
             bytes_accessed=2 * columns * width + 4 * rows * columns),
-    )(configs.reshape(chunks, rows, width), weights.reshape(1, width))
+    )(configs.reshape(chunks, rows, width), weights)
 
 
 def solution(mesh):

time: 311 us -> 292 us (0.939); the launches traced: 308 us -> 292 us
  Pallas kernels: 298 us -> 284 us
    pallas_call x1, Pallas kernels: 298 us -> 284 us  [local(): pl.pallas_call(functools.partial(kernel, nq, nc), out_shape=jax.ShapeDtyp...]
where the time goes in v2:
time: 292 us
  Pallas kernels  284 us (97%)
  local copies, waits for them, and re-layouts  7.89 us (3%)
    pallas_call x1, Pallas kernels, local(): pl.pallas_call(functools.partial(kernel, nq, nc), out_shape=jax.ShapeDtyp...  284 us
    unnamed x1, local copies, waits for them, and re-layouts  7.89 us

profile of v2, /device:TPU:24, one launch (start us, length us, event | category | flops | bytes accessed | tf_op | source)
XLA Modules:
  0.0 291.8 jit_solution(12488429288280106359)
XLA Ops:
  0.0 283.9 %shard_map.28 = f32[1024,2048]{1,0:T(8,128)} custom-call(bf16[2,1024,768]{2,1,0:T(8,128)(2,1)} %bitcast.1, f32[768]{0:T(1024)} %w_ref.1), custom_call_target="tpu_custom_call" | custom-call | flops 25769803776 | bytes 11534336 | tf_op jit(solution)/shard_map/pallas_call | solution.py:226
  283.9 7.9 %copy.4 = f32[1024,2048]{1,0:T(8,128)} copy(f32[1024,2048]{1,0:T(8,128)} %shard_map.28) | data formatting | bytes 16777216

commit v3 on v1

v3 whole, which is shorter than its diff:
```python
import functools

import jax
import jax.numpy as jnp
from jax import lax
from jax.experimental import pallas as pl
from jax.experimental.pallas import tpu as pltpu
from jax.sharding import PartitionSpec as P

MESH = pl.DeviceIdType.MESH


def visit(z, k, nz):
    below, above = z, nz - 1 - z
    pairs = jnp.minimum(below, above)
    paired = k <= 2 * pairs
    step = jnp.where(paired, (k + 1) // 2, k - pairs)
    down = jnp.where(paired, k % 2 == 1, below > above)
    return jnp.where(down, z - step, z + step)


def kernel(nq, nc, x_ref, w_ref, out_ref, held, left, wts, scaled,
           load_sem, recv_sem, line_sem, own_sem, pair_sem, cross_sem, left_recv, left_send, w_recv, w_send):
    chunks, rows, _ = x_ref.shape
    nz = nq // 2
    q, c = lax.axis_index("quad"), lax.axis_index("conf")
    z, x = q // 2, q % 2
    root, mine = q // chunks, q % chunks
    buddy = z + 1 - 2 * (z % 2)
    bits = nc.bit_length() - 1
    far = 0
    for b in range(bits):
        far = far + (((c // 2**b) % 2 + (root // 2**b) % 2) % 2) * 2**b

    load = pltpu.make_async_copy(x_ref, held.at[q], load_sem)
    load.start()
    barrier = pltpu.get_barrier_semaphore()
    for k in range(1, nq):
        pl.semaphore_signal(barrier, inc=1, device_id={"quad": lax.rem(q + k, nq)}, device_id_type=MESH)
    for k in range(1, nc):
        pl.semaphore_signal(barrier, inc=1, device_id={"conf": lax.rem(c + k, nc)}, device_id_type=MESH)
    wts[q] = jnp.broadcast_to(w_ref[...].reshape(1, -1), wts.shape[1:])
    load.wait()
    pl.semaphore_wait(barrier, nq + nc - 2)

    parts, half = 2 * chunks, rows // 2

    def view(ref, sub):
        return ref.at[pl.ds(sub * half, half)]

    def turn(i, source):
        return (i // 2 + 1 - source) % chunks

    def along(slot, i, source, to, sem):
        block = view(held.at[slot, turn(i, source)], i % 2)
        return pltpu.make_async_remote_copy(
            src_ref=block, dst_ref=block, send_sem=sem,
            recv_sem=recv_sem.at[slot, i], device_id={"quad": to}, device_id_type=MESH)

    def line_copy(at, i, to):
        return along(2 * at + x, i, x, to, line_sem.at[at, i])

    def own_copy(i, to):
        return along(q, i, x, to, own_sem.at[i])

    def pair_copy(at, i):
        return along(2 * at + x, i, x, 2 * z + 1 - x, pair_sem.at[at, i])

    def cross_copy(at, i):
        return along(2 * at + 1 - x, i, 1 - x, 2 * buddy + x, cross_sem.at[i - parts // 2])

    def paired(at, i):
        return jnp.logical_or(at != buddy, i < parts // 2)

    def left_copy(src, slot, sub, b):
        bit = (c // 2**b) % 2
        return pltpu.make_async_remote_copy(
            src_ref=view(src, sub), dst_ref=view(left.at[slot], sub), send_sem=left_send.at[slot, sub, b],
            recv_sem=left_recv.at[slot, sub], device_id={"conf": c + (1 - 2 * bit) * 2**b}, device_id_type=MESH)

    def weight_copy(k):
        return pltpu.make_async_remote_copy(
            src_ref=wts.at[q], dst_ref=wts.at[q], send_sem=w_send.at[k],
            recv_sem=w_recv.at[q], device_id={"quad": lax.rem(q + k, nq)}, device_id_type=MESH)

    def pass_left(src, slot, sub, here):
        for b in reversed(range(bits)):
            @pl.when(jnp.logical_and(here, far % 2 ** (b + 1) == 0))
            def _():
                left_copy(src, slot, sub, b).start()

    def root_sends(slot, i, source):
        ch = turn(i, source)
        pass_left(held.at[slot, ch], slot, i % 2, jnp.logical_and(far == 0, ch == mine))

    for i in range(parts):
        @pl.when(z < nz - 1)
        def _():
            line_copy(z, i, q + 2).start()

        @pl.when(z > 0)
        def _():
            own_copy(i, q - 2).start()

        pair_copy(z, i).start()
        root_sends(q, i, x)
    for k in range(1, nq):
        weight_copy(k).start()

    out_ref[...] = jnp.zeros_like(out_ref)

    def multiply(slot, ch=None, again=False):
        if not again:
            @pl.when(slot != q)
            def _():
                pltpu.make_async_remote_copy(
                    src_ref=wts.at[slot], dst_ref=wts.at[slot], send_sem=w_send.at[0],
                    recv_sem=w_recv.at[slot], device_id={"quad": lax.rem(q + 1, nq)},
                    device_id_type=MESH).wait_recv()

            @pl.when(far != 0)
            def _():
                for sub in range(2):
                    left_copy(left.at[slot], slot, sub, 0).wait_recv()
                    pass_left(left.at[slot], slot, sub, True)

        scale = wts[slot, 0:1, :]

        @pl.when(far != 0)
        def _():
            scaled[...] = (left[slot].astype(jnp.float32) * scale).astype(jnp.bfloat16)

        @pl.when(far == 0)
        def _():
            scaled[...] = (held[slot, mine].astype(jnp.float32) * scale).astype(jnp.bfloat16)

        tile = min(256, rows)
        for block in range(chunks) if ch is None else [ch]:
            across = pl.ds(pl.multiple_of(block * rows, rows), rows)

            @pl.loop(0, rows // tile)
            def _(t):
                part = pl.ds(pl.multiple_of(t * tile, tile), tile)
                out_ref[part, across] += lax.dot_general(
                    scaled[part, :], held[slot, block], (((1,), (1,)), ((), ())),
                    preferred_element_type=jnp.float32)

    def take_line(at, i):
        line_copy(at, i, q).wait_recv()

        @pl.when(jnp.logical_and(at < z, z < nz - 1))
        def _():
            line_copy(at, i, q + 2).start()

        @pl.when(jnp.logical_and(at > z, z > 0))
        def _():
            line_copy(at, i, q - 2).start()

        @pl.when(paired(at, i))
        def _():
            pair_copy(at, i).start()

        root_sends(2 * at + x, i, x)

    def take_pair(at, i):
        @pl.when(paired(at, i))
        def _():
            along(2 * at + 1 - x, i, 1 - x, q, cross_sem.at[0]).wait_recv()
            root_sends(2 * at + 1 - x, i, 1 - x)

    def multiply_other(at):
        @pl.when(at != buddy)
        def _():
            multiply(2 * at + 1 - x)

    @pl.loop(1, nz)
    def _(k):
        at, before = visit(z, k, nz), visit(z, k - 1, nz)
        for i in range(parts):
            take_line(at, i)
            take_pair(before, i)
        multiply(2 * before + x)

        @pl.when(k >= 2)
        def _():
            multiply_other(visit(z, jnp.maximum(k - 2, 0), nz))

    end = visit(z, nz - 1, nz)
    for i in range(parts // 2):
        take_pair(end, i)
    for i in range(parts // 2, parts):
        cross_copy(z, i).start()
    multiply(2 * end + x)
    multiply_other(visit(z, nz - 2, nz))

    last, crossed = 2 * end + 1 - x, 2 * buddy + 1 - x
    split = chunks == 2 and nz > 2
    if split:
        multiply(crossed, turn(0, 1 - x))
        multiply(last, turn(0, 1 - x))
    for i in range(parts // 2, parts):
        take_pair(end, i)
    if split:
        multiply(last, turn(parts - 1, 1 - x), again=True)
    else:
        multiply_other(end)
    for i in range(parts // 2, parts):
        cross_copy(buddy, i).wait_recv()
        root_sends(crossed, i, 1 - x)
    if split:
        multiply(crossed, turn(parts - 1, 1 - x), again=True)
    else:
        multiply(crossed)

    for i in range(parts // 2, parts):
        cross_copy(z, i).wait_send()

    for i in range(parts):
        @pl.when(z > 0)
        def _():
            own_copy(i, q - 2).wait_send()

    @pl.loop(0, nz)
    def _(at):
        sent = jnp.logical_or(jnp.logical_and(at <= z, z < nz - 1), jnp.logical_and(at > z, z > 0))
        for i in range(parts):
            @pl.when(sent)
            def _():
                line_copy(at, i, q).wait_send()

            @pl.when(paired(at, i))
            def _():
                pair_copy(at, i).wait_send()

    @pl.loop(0, nq)
    def _(slot):
        for b in range(bits):
            @pl.when(far % 2 ** (b + 1) == 0)
            def _():
                for sub in range(2):
                    left_copy(left.at[slot], slot, sub, b).wait_send()

    for k in range(1, nq):
        weight_copy(k).wait_send()


def local(nq, nc, configs, weights):
    columns, width = configs.shape
    rows = columns * nc // nq
    chunks = columns // rows
    dma = pltpu.SemaphoreType.DMA
    bits = nc.bit_length() - 1
    return pl.pallas_call(
        functools.partial(kernel, nq, nc),
        out_shape=jax.ShapeDtypeStruct((rows, columns), jnp.float32),
        in_specs=[pl.BlockSpec(memory_space=pl.ANY), pl.BlockSpec(memory_space=pltpu.VMEM)],
        out_specs=pl.BlockSpec(memory_space=pltpu.VMEM),
        scratch_shapes=[
            pltpu.VMEM((nq, chunks, rows, width), jnp.bfloat16),
            pltpu.VMEM((nq, rows, width), jnp.bfloat16),
            pltpu.VMEM((nq, 8, width), jnp.float32),
            pltpu.VMEM((rows, width), jnp.bfloat16),
            dma,
            dma((nq, 2 * chunks)),
            dma((nq // 2, 2 * chunks)),
            dma((2 * chunks,)),
            dma((nq // 2, 2 * chunks)),
            dma((chunks,)),
            dma((nq, 2)),
            dma((nq, 2, bits)),
            dma((nq,)),
            dma((nq,)),
        ],
        compiler_params=pltpu.CompilerParams(
            collective_id=0, has_side_effects=True, vmem_limit_bytes=60 * 2**20),
        cost_estimate=pl.CostEstimate(
            flops=2 * rows * columns * width * nq, transcendentals=0,
            bytes_accessed=2 * columns * width + 4 * rows * columns),
    )(configs.reshape(chunks, rows, width), weights)


def solution(mesh):
    return jax.shard_map(
        functools.partial(local, mesh.shape["quad"], mesh.shape["conf"]),
        mesh=mesh,
        in_specs=(P("conf", "quad"), P("quad")),
        out_specs=P("quad", "conf"),
        check_vma=False,
    )
```

time: 311 us -> 282 us (0.907)
  Pallas kernels: 298 us -> 269 us
    pallas_call x1, Pallas kernels: 298 us -> 269 us  [local(): pl.pallas_call(functools.partial(kernel, nq, nc), out_shape=jax.ShapeDtyp...]
where the time goes in v3:
time: 282 us; the launch traced here: 277 us
  Pallas kernels  269 us (95%)
  local copies, waits for them, and re-layouts  7.89 us (3%)
    pallas_call x1, Pallas kernels, local(): pl.pallas_call(functools.partial(kernel, nq, nc), out_shape=jax.ShapeDtyp...  269 us
    unnamed x1, local copies, waits for them, and re-layouts  7.89 us

profile of v3, /device:TPU:24, one launch (start us, length us, event | category | flops | bytes accessed | tf_op | source)
XLA Modules:
  0.0 277.2 jit_solution(13957432639045847481)
XLA Ops:
  0.0 269.3 %shard_map.28 = f32[1024,2048]{1,0:T(8,128)} custom-call(bf16[2,1024,768]{2,1,0:T(8,128)(2,1)} %bitcast.1, f32[768]{0:T(1024)} %w_ref.1), custom_call_target="tpu_custom_call" | custom-call | flops 25769803776 | bytes 11534336 | tf_op jit(solution)/shard_map/pallas_call | solution.py:253
  269.3 7.9 %copy.4 = f32[1024,2048]{1,0:T(8,128)} copy(f32[1024,2048]{1,0:T(8,128)} %shard_map.28) | data formatting | bytes 16777216

commit v4 on v3

--- a/solution.py
+++ b/solution.py
@@ -67,10 +67,13 @@
         return along(2 * at + x, i, x, 2 * z + 1 - x, pair_sem.at[at, i])
 
     def cross_copy(at, i):
-        return along(2 * at + 1 - x, i, 1 - x, 2 * buddy + x, cross_sem.at[i - parts // 2])
+        return along(2 * at + 1 - x, i, 1 - x, 2 * buddy + x, cross_sem.at[i])
 
     def paired(at, i):
-        return jnp.logical_or(at != buddy, i < parts // 2)
+        return jnp.logical_or(at != buddy, jnp.logical_and(i < parts // 2, jnp.logical_not(at_end(buddy))))
+
+    def at_end(at):
+        return jnp.logical_or(at == 0, at == nz - 1)
 
     def left_copy(src, slot, sub, b):
         bit = (c // 2**b) % 2
@@ -179,22 +182,39 @@
         for i in range(parts):
             take_line(at, i)
             take_pair(before, i)
-        multiply(2 * before + x)
-
-        @pl.when(k >= 2)
-        def _():
-            multiply_other(visit(z, jnp.maximum(k - 2, 0), nz))
+            if i == parts // 2 - 1:
+                multiply(2 * before + x)
+
+                @pl.when(k >= 2)
+                def _():
+                    multiply_other(visit(z, jnp.maximum(k - 2, 0), nz))
+
+        @pl.when(jnp.logical_and(k == 1, at_end(z)))
+        def _():
+            for i in range(parts):
+                cross_copy(z, i).start()
 
     end = visit(z, nz - 1, nz)
     for i in range(parts // 2):
         take_pair(end, i)
-    for i in range(parts // 2, parts):
-        cross_copy(z, i).start()
+
+    @pl.when(jnp.logical_not(at_end(z)))
+    def _():
+        for i in range(parts // 2, parts):
+            cross_copy(z, i).start()
+
     multiply(2 * end + x)
     multiply_other(visit(z, nz - 2, nz))
 
     last, crossed = 2 * end + 1 - x, 2 * buddy + 1 - x
     split = chunks == 2 and nz > 2
+
+    @pl.when(at_end(buddy))
+    def _():
+        for i in range(parts // 2):
+            cross_copy(buddy, i).wait_recv()
+            root_sends(crossed, i, 1 - x)
+
     if split:
         multiply(crossed, turn(0, 1 - x))
         multiply(last, turn(0, 1 - x))
@@ -212,8 +232,10 @@
     else:
         multiply(crossed)
 
-    for i in range(parts // 2, parts):
-        cross_copy(z, i).wait_send()
+    for i in range(parts):
+        @pl.when(jnp.logical_or(i >= parts // 2, at_end(z)))
+        def _():
+            cross_copy(z, i).wait_send()
 
     for i in range(parts):
         @pl.when(z > 0)
@@ -265,7 +287,7 @@
             dma((nq // 2, 2 * chunks)),
             dma((2 * chunks,)),
             dma((nq // 2, 2 * chunks)),
-            dma((chunks,)),
+            dma((2 * chunks,)),
             dma((nq, 2)),
             dma((nq, 2, bits)),
             dma((nq,)),

time: 282 us -> 264 us (0.936)
  Pallas kernels: 269 us -> 253 us
    pallas_call x1, Pallas kernels: 269 us -> 253 us  [local(): pl.pallas_call(functools.partial(kernel, nq, nc), out_shape=jax.ShapeDtyp...]
where the time goes in v4:
time: 264 us; the launch traced here: 261 us
  Pallas kernels  253 us (96%)
  local copies, waits for them, and re-layouts  7.89 us (3%)
    pallas_call x1, Pallas kernels, local(): pl.pallas_call(functools.partial(kernel, nq, nc), out_shape=jax.ShapeDtyp...  253 us
    unnamed x1, local copies, waits for them, and re-layouts  7.89 us

profile of v4, /device:TPU:24, one launch (start us, length us, event | category | flops | bytes accessed | tf_op | source)
XLA Modules:
  0.0 260.9 jit_solution(15633355999267387430)
XLA Ops:
  0.0 253.0 %shard_map.28 = f32[1024,2048]{1,0:T(8,128)} custom-call(bf16[2,1024,768]{2,1,0:T(8,128)(2,1)} %bitcast.1, f32[768]{0:T(1024)} %w_ref.1), custom_call_target="tpu_custom_call" | custom-call | flops 25769803776 | bytes 11534336 | tf_op jit(solution)/shard_map/pallas_call | solution.py:275
  253.0 7.9 %copy.4 = f32[1024,2048]{1,0:T(8,128)} copy(f32[1024,2048]{1,0:T(8,128)} %shard_map.28) | data formatting | bytes 16777216

commit v5 on v4

--- a/solution.py
+++ b/solution.py
@@ -112,7 +112,7 @@
 
     out_ref[...] = jnp.zeros_like(out_ref)
 
-    def multiply(slot, ch=None, again=False):
+    def multiply(slot, ch=None, again=False, keep=0):
         if not again:
             @pl.when(slot != q)
             def _():
@@ -129,13 +129,13 @@
 
         scale = wts[slot, 0:1, :]
 
-        @pl.when(far != 0)
-        def _():
-            scaled[...] = (left[slot].astype(jnp.float32) * scale).astype(jnp.bfloat16)
-
-        @pl.when(far == 0)
-        def _():
-            scaled[...] = (held[slot, mine].astype(jnp.float32) * scale).astype(jnp.bfloat16)
+        @pl.when(jnp.logical_and(far != 0, not again))
+        def _():
+            scaled[keep] = (left[slot].astype(jnp.float32) * scale).astype(jnp.bfloat16)
+
+        @pl.when(jnp.logical_and(far == 0, not again))
+        def _():
+            scaled[keep] = (held[slot, mine].astype(jnp.float32) * scale).astype(jnp.bfloat16)
 
         tile = min(256, rows)
         for block in range(chunks) if ch is None else [ch]:
@@ -145,7 +145,7 @@
             def _(t):
                 part = pl.ds(pl.multiple_of(t * tile, tile), tile)
                 out_ref[part, across] += lax.dot_general(
-                    scaled[part, :], held[slot, block], (((1,), (1,)), ((), ())),
+                    scaled[keep, part, :], held[slot, block], (((1,), (1,)), ((), ())),
                     preferred_element_type=jnp.float32)
 
     def take_line(at, i):
@@ -216,7 +216,7 @@
             root_sends(crossed, i, 1 - x)
 
     if split:
-        multiply(crossed, turn(0, 1 - x))
+        multiply(crossed, turn(0, 1 - x), keep=1)
         multiply(last, turn(0, 1 - x))
     for i in range(parts // 2, parts):
         take_pair(end, i)
@@ -228,7 +228,7 @@
         cross_copy(buddy, i).wait_recv()
         root_sends(crossed, i, 1 - x)
     if split:
-        multiply(crossed, turn(parts - 1, 1 - x), again=True)
+        multiply(crossed, turn(parts - 1, 1 - x), again=True, keep=1)
     else:
         multiply(crossed)
 
@@ -281,7 +281,7 @@
             pltpu.VMEM((nq, chunks, rows, width), jnp.bfloat16),
             pltpu.VMEM((nq, rows, width), jnp.bfloat16),
             pltpu.VMEM((nq, 8, width), jnp.float32),
-            pltpu.VMEM((rows, width), jnp.bfloat16),
+            pltpu.VMEM((2, rows, width), jnp.bfloat16),
             dma,
             dma((nq, 2 * chunks)),
             dma((nq // 2, 2 * chunks)),

time: 264 us -> 263 us (level)
  no operation moved by 1% of the time
where the time goes in v5:
time: 263 us; the launch traced here: 260 us
  Pallas kernels  252 us (96%)
  local copies, waits for them, and re-layouts  7.89 us (3%)
    pallas_call x1, Pallas kernels, local(): pl.pallas_call(functools.partial(kernel, nq, nc), out_shape=jax.ShapeDtyp...  252 us
    unnamed x1, local copies, waits for them, and re-layouts  7.89 us

profile of v5, /device:TPU:24, one launch (start us, length us, event | category | flops | bytes accessed | tf_op | source)
XLA Modules:
  0.0 260.3 jit_solution(11847813194580603833)
XLA Ops:
  0.0 252.4 %shard_map.28 = f32[1024,2048]{1,0:T(8,128)} custom-call(bf16[2,1024,768]{2,1,0:T(8,128)(2,1)} %bitcast.1, f32[768]{0:T(1024)} %w_ref.1), custom_call_target="tpu_custom_call" | custom-call | flops 25769803776 | bytes 11534336 | tf_op jit(solution)/shard_map/pallas_call | solution.py:275
  252.4 7.9 %copy.4 = f32[1024,2048]{1,0:T(8,128)} copy(f32[1024,2048]{1,0:T(8,128)} %shard_map.28) | data formatting | bytes 16777216
